TPU v7x, 32 devices: a whole 2x2x4 slice. The times are simulated.
32 devices in a mesh: member: 4 (over x, core), shard: 8 (over z, y).
Axes of the slice: x: 2, y: 2, z: 4, core: 2. Of those that a mesh axis runs over, the one named last changes fastest.
Arguments:
- latent: bfloat16 [4, 256, 1024], P('member', 'shard'), may hold values from -6 to 6
- grid_embed: bfloat16 [2048, 1024], P('shard'), may hold values from -6 to 6
- edge_src: int32 [2048, 3], P('shard'), may hold values from 0 to 255, as said below
- area: float32 [2048], P('shard'), may hold values from 0.15 to 27
- target: float32 [2048, 100], P('shard'), may hold values from -6 to 6
- w_query: bfloat16 [1024, 1024], replicated, may hold values from -0.1875 to 0.1875
- w_keyval: bfloat16 [1024, 2048], replicated, may hold values from -0.1875 to 0.1875
- w_head: bfloat16 [1024, 100], replicated, may hold values from -0.1875 to 0.1875
Outputs:
- loss: float32 [4], P('member')
- d_latent: float32 [4, 256, 1024], P('member', 'shard')
- grad_query: float32 [1024, 1024], P('shard')
- grad_keyval: float32 [1024, 2048], P('shard')
- grad_head: float32 [1024, 100], P('shard')
Inputs may be any that keep to these rules, and one draw needn't show every extreme that they name: edge_src[g, k] is a node of the latent block of index g // 256 or of one of the two blocks beside it, cyclically, where block b holds nodes b * 32 to (b + 1) * 32 - 1.
All inputs are finite; a program needn't handle non-finite values.
Results may differ from a plain program's by a relative error of at most 0.035.
Values may be sent and summed in bfloat16 or wider, within the bound.
A program may use at most 128 MiB of HBM per device.

v0:
```python
import math

import jax
import jax.numpy as jnp
from jax import lax
from jax.sharding import PartitionSpec as P

HEADS = 16
KNB = 3


def padded(cells, sides, width):
    for axis, dim in sides:
        count = lax.axis_size(axis)
        head = lax.slice_in_dim(cells, 0, width, axis=dim)
        tail = lax.slice_in_dim(cells, cells.shape[dim] - width, cells.shape[dim], axis=dim)
        cells = jnp.concatenate(
            [
                lax.ppermute(tail, axis, [(i, (i + 1) % count) for i in range(count)]),
                cells,
                lax.ppermute(head, axis, [((i + 1) % count, i) for i in range(count)]),
            ],
            axis=dim,
        )
    return cells


def from_behind(array, axis, by):
    devices = lax.axis_size(axis)
    return lax.ppermute(array, axis, [(i, (i + by) % devices) for i in range(devices)])


def normalize_heads(values):
    shaped = values.reshape(values.shape[:-1] + (HEADS, values.shape[-1] // HEADS))
    return shaped * lax.rsqrt(jnp.mean(shaped * shaped, -1, keepdims=True) + 1e-06)


def attend(query, table, source):
    width = query.shape[-1]
    size = width // HEADS
    picked = table[source]
    query_norm = normalize_heads(query)
    key_norm = normalize_heads(picked[..., :width])
    values = picked[..., width:].reshape(picked.shape[:2] + (HEADS, size))
    score = jnp.einsum("bhs,bkhs->bhk", query_norm, key_norm) * size ** (-0.5)
    expon = jnp.exp(score)
    weight = expon / jnp.sum(expon, -1, keepdims=True)
    return jnp.einsum("bhk,bkhs->bhs", weight, values).reshape(query.shape)


def layer_norm(hidden):
    center = hidden - jnp.mean(hidden, -1, keepdims=True)
    return center * lax.rsqrt(jnp.mean(center * center, -1, keepdims=True) + 1e-05)


def smooth_abs(delta):
    return jnp.sqrt(delta * delta + 0.0625)


def slope(delta):
    return delta / smooth_abs(delta)


def inner_rows(left, right):
    return lax.dot_general(
        left, right, (((0,), (0,)), ((), ())), preferred_element_type=jnp.float32
    )


def on_device(latent, grid_embed, edge_src, area, target, w_query, w_keyval, w_head):
    rows = grid_embed.shape[0]
    width = grid_embed.shape[1]
    nodes = latent.shape[1]
    shards = lax.axis_size("shard")
    members = lax.axis_size("member")
    own_latent = latent[0]
    here = lax.axis_index("shard")
    source = jnp.mod(edge_src - (here - 1) * nodes, shards * nodes)
    widened = padded(own_latent, (("shard", 0),), nodes)
    table_low = jnp.dot(widened, w_keyval, preferred_element_type=jnp.float32).astype(jnp.bfloat16)
    table = lax.optimization_barrier(table_low).astype(jnp.float32)
    block = math.gcd(rows, 512)
    blocks = rows // block
    query = jnp.dot(grid_embed, w_query, preferred_element_type=jnp.float32)
    query_blocks = query.reshape(blocks, block, width)
    source_blocks = source.reshape(blocks, block, KNB)
    mixed = lax.map(lambda pair: attend(pair[0], table, pair[1]), (query_blocks, source_blocks))
    hidden = grid_embed.astype(jnp.float32) + mixed.reshape(rows, width)
    normed = layer_norm(hidden).astype(jnp.bfloat16)
    preds = jnp.dot(normed, w_head, preferred_element_type=jnp.float32)
    variables = preds.shape[1]
    pair_scale = 1.0 / (members * (members - 1))
    divisor = rows * shards * variables
    empty = jnp.zeros(preds.shape, jnp.float32)
    carry = (empty, empty)
    delta = preds[None] - lax.all_gather(
        preds[None].astype(jnp.bfloat16), "member", axis=0, tiled=True
    ).astype(jnp.float32)
    pair_value = carry[0] + jnp.sum(smooth_abs(delta), 0)
    pair_slope = carry[1] + jnp.sum(slope(delta), 0)
    miss = preds - target
    weights = area[:, None]
    local_loss = jnp.sum(
        weights * (smooth_abs(miss) / members - 0.5 * pair_scale * (pair_value - 0.25))
    )
    loss = lax.psum(local_loss[None], "shard") / divisor
    d_pred = weights * (slope(miss) / members - pair_scale * pair_slope)
    d_outb = d_pred.astype(jnp.bfloat16)
    d_normed = jnp.dot(d_outb, w_head.T, preferred_element_type=jnp.float32)
    ignored, norm_back = jax.vjp(layer_norm, hidden)
    d_hidden = norm_back(d_normed)[0]

    def block_back(carry, items):
        query_part, source_part, d_part = items
        ignored_out, attend_back = jax.vjp(
            lambda qq, tt: attend(qq, tt, source_part), query_part, table
        )
        d_q, d_t = attend_back(d_part)
        return (carry + d_t, d_q)

    d_table, d_query = lax.scan(
        block_back,
        jnp.zeros(table.shape, jnp.float32),
        (query_blocks, source_blocks, d_hidden.reshape(blocks, block, width)),
    )
    d_queryb = d_query.reshape(rows, width).astype(jnp.bfloat16)
    from_upper = from_behind(d_table[:nodes].astype(jnp.bfloat16), "shard", -1).astype(jnp.float32)
    from_lower = from_behind(d_table[2 * nodes :].astype(jnp.bfloat16), "shard", 1).astype(
        jnp.float32
    )
    d_own = d_table[nodes : 2 * nodes] + from_upper + from_lower
    d_ownb = d_own.astype(jnp.bfloat16)
    d_latent = jnp.dot(d_ownb, w_keyval.T, preferred_element_type=jnp.float32)[None]
    scale = (members * rows * shards) ** (-0.5)
    pick = lambda data: data
    parts = [
        inner_rows(pick(grid_embed), d_queryb),
        inner_rows(pick(own_latent), d_ownb),
        inner_rows(pick(normed), d_outb),
    ]
    portion = lax.psum_scatter(
        (jnp.concatenate(parts, axis=1) * scale).astype(jnp.bfloat16),
        "shard",
        scatter_dimension=0,
        tiled=True,
    )
    total = lax.psum(portion, "member").astype(jnp.float32)
    return (loss, d_latent, total[:, :width], total[:, width : 3 * width], total[:, 3 * width :])


def solution(mesh):
    placed = (
        P("member", "shard", None),
        P("shard", None),
        P("shard", None),
        P("shard"),
        P("shard", None),
        P(),
        P(),
        P(),
    )
    return jax.shard_map(
        on_device,
        mesh=mesh,
        in_specs=placed,
        out_specs=(
            P("member"),
            P("member", "shard", None),
            P("shard", None),
            P("shard", None),
            P("shard", None),
        ),
        check_vma=False,
    )
```

profile of v0, /device:TPU:0, one launch (start us, length us, event | category | flops | bytes accessed | tf_op | source)
XLA Modules:
  0.0 337.3 jit_solution(13514113283399120255)
XLA Ops:
  7.2 6.1 %collective-permute-start.1 = (bf16[32,1024]{1,0:T(8,128)(2,1)}, bf16[32,1024]{1,0:T(8,128)(2,1)S(1)}, u32[]{:S(2)}, u32[]{:S(2)}) collective-permute-start(bf16[32,1024]{1,0:T(8,128)(2,1)} %bitcast.70), channel_id=1, source_target_pairs={{1,0},{2,1},{3,2},{4,3},{5,4},{6,5},{7,6},{0,7},{9,8},{10,9},{11,1... | collective-permute-start | bytes 196616 | tf_op jit(solution)/shard_map/ppermute | solution.py:21
  17.8 2.7 collective-permute-done
  21.4 4.3 %gather_fusion.1 = bf16[768,2048]{1,0:T(8,128)(2,1)} fusion(bf16[96,2048]{1,0:T(8,128)(2,1)S(1)} %convolution_convert_fusion, s32[1024]{0:T(1024)S(1)} %pad_clamp_fusion), kind=kCustom, calls=%fused_computation.1 | custom fusion | bytes 6294528 | tf_op jit(solution)/shard_map/while/body/eval_jaxpr/gather | solution.py:41
  25.7 5.0 %gather_fusion = f32[768,2048]{1,0:T(8,128)} fusion(f32[96,2048]{1,0:T(8,128)S(1)} %convert_element_type.49, s32[1024]{0:T(1024)S(1)} %pad_clamp_fusion), kind=kCustom, calls=%fused_computation | custom fusion | bytes 12585984 | tf_op jit(solution)/shard_map/while/body/eval_jaxpr/gather | solution.py:41
  30.7 10.5 %reshape.145 = f32[256,3,2048]{2,1,0:T(4,128)} reshape(f32[768,2048]{1,0:T(8,128)} %gather_fusion) | data formatting | bytes 12582912 | tf_op jit(solution)/shard_map/while/body/eval_jaxpr/gather | solution.py:41
  41.2 5.1 %slice.44 = f32[256,3,1024]{2,1,0:T(4,128)} slice(f32[256,3,2048]{2,1,0:T(4,128)} %reshape.145), slice={[0:256], [0:3], [0:1024]} | slice | bytes 6291456 | tf_op jit(solution)/shard_map/while/body/eval_jaxpr/slice | solution.py:43
  46.3 3.4 %copy.26 = f32[256,3,1024]{0,2,1:T(8,128)S(1)} copy(f32[256,3,1024]{2,1,0:T(4,128)} %slice.44) | data formatting | bytes 6291456 | tf_op jit(solution)/shard_map/while/body/eval_jaxpr/slice | solution.py:43
  52.4 9.1 %reshape.153 = bf16[256,3,2048]{2,1,0:T(4,128)(2,1)} reshape(bf16[768,2048]{1,0:T(8,128)(2,1)} %gather_fusion.1) | data formatting | bytes 6291456 | tf_op jit(solution)/shard_map/while/body/eval_jaxpr/gather | solution.py:41
  61.5 3.6 %slice.45 = bf16[256,3,1024]{2,1,0:T(4,128)(2,1)} slice(bf16[256,3,2048]{2,1,0:T(4,128)(2,1)} %reshape.153), slice={[0:256], [0:3], [1024:2048]} | slice | bytes 3145728 | tf_op jit(solution)/shard_map/while/body/eval_jaxpr/slice | solution.py:44
  65.2 4.1 %copy.56 = bf16[256,3,1024]{0,2,1:T(8,128)(2,1)} copy(bf16[256,3,1024]{2,1,0:T(4,128)(2,1)} %slice.45) | data formatting | bytes 3145728
  69.3 2.9 multiply_reduce_fusion.2
  80.5 6.3 %all-gather = bf16[1024,100]{0,1:T(8,128)(2,1)} all-gather(bf16[256,100]{0,1:T(8,128)(2,1)S(1)} %get-tuple-element.68), channel_id=2, replica_groups=mesh['member'=4,'shard'=8] {'member'}, dimensions={0}, use_global_device_ids=true | all-gather | bytes 256000 | tf_op jit(solution)/shard_map/all_gather | solution.py:96
  97.7 2.5 broadcast_multiply_fusion
  103.5 3.1 pad_add_fusion
  106.6 9.6 %copy.30 = f32[256,3,2048]{2,1,0:T(4,128)} copy(f32[256,3,2048]{0,2,1:T(8,128)} %pad_add_fusion) | data formatting | bytes 12582912 | tf_op jit(solution)/shard_map/while/body/eval_jaxpr/transpose(jvp())/add_any | solution.py:43
  116.3 10.8 %reshape.164 = f32[768,2048]{1,0:T(8,128)} reshape(f32[256,3,2048]{2,1,0:T(4,128)} %copy.30) | data formatting | bytes 12582912 | tf_op jit(solution)/shard_map/while/body/eval_jaxpr/transpose(jvp())/add_any | solution.py:43
  127.1 14.9 %scatter_custom_fusion = f32[96,2048]{1,0:T(8,128)S(1)} fusion(s32[768]{0:T(1024)} %copy-done.34, f32[768,2048]{1,0:T(8,128)} %reshape.164, f32[]{:T(128)} %constant.61.clone.1), kind=kCustom, calls=%fused_computation.35 | custom fusion | flops 1572864 | bytes 786944 | tf_op jit(solution)/shard_map/while/body/eval_jaxpr/transpose(jvp())/scatter-add | solution.py:41
  147.9 4.5 %collective-permute-done.3 = bf16[32,2048]{1,0:T(8,128)(2,1)S(1)} collective-permute-done((bf16[32,2048]{1,0:T(8,128)(2,1)S(1)}, bf16[32,2048]{1,0:T(8,128)(2,1)S(1)}, u32[]{:S(2)}, u32[]{:S(2)}) %collective-permute-start.3) | collective-permute-done | bytes 131104 | tf_op jit(solution)/shard_map/ppermute | solution.py:30
  153.7 4.2 %fusion = bf16[1024,3172]{0,1:T(8,128)(2,1)} fusion(f32[1024,100]{0,1:T(8,128)S(1)} %fusion.27, f32[1024,2048]{0,1:T(8,128)S(1)} %convolution_bitcast_fusion, f32[1024,1024]{0,1:T(8,128)S(1)} %convolution_bitcast_fusion.1), kind=kLoop, calls=%fused_computation.4 | loop fusion | flops 12992512 | bytes 19488768 | tf_op jit(solution)/shard_map/convert_element_type | solution.py:142
  157.9 9.3 %copy.58 = bf16[1024,3172]{1,0:T(8,128)(2,1)} copy(bf16[1024,3172]{0,1:T(8,128)(2,1)} %fusion) | data formatting | bytes 12992512
  167.2 119.5 %reduce-scatter.4.cloned.1.call-done = bf16[128,3172]{1,0:T(8,128)(2,1)} async-done(((bf16[1024,3172]{1,0:T(8,128)(2,1)}), bf16[128,3172]{1,0:T(8,128)(2,1)}) %reduce-scatter.4.cloned.1.call-update) | async-done | bytes 812048
  288.9 20.2 %psum.14 = f32[1]{0:T(128)} all-reduce(f32[1]{0:T(128)} %bitcast.11), channel_id=1, replica_groups=mesh['member'=4,'shard'=8] {'shard'}, use_global_device_ids=true, to_apply=%region_7.8 | all-reduce | flops 1 | bytes 8 | tf_op jit(solution)/shard_map/psum | solution.py:106
  309.7 4.4 %convolution_bitcast_fusion.2 = f32[1,32,1024]{2,1,0:T(8,128)} fusion(bf16[32,2048]{1,0:T(8,128)(2,1)S(1)} %fusion.9, bf16[1024,2048]{1,0:T(8,128)(2,1)} %param.14), kind=kOutput, calls=%fused_computation.21 | convolution fusion | flops 134217728 | bytes 4456448 | tf_op jit(solution)/shard_map/dot_general | solution.py:133
  314.1 9.5 %all-reduce.4.cloned.1.call-done = bf16[128,3172]{0,1:T(8,128)(2,1)} async-done(((bf16[128,3172]{0,1:T(8,128)(2,1)}), bf16[128,3172]{0,1:T(8,128)(2,1)}) %all-reduce.4.cloned.1.call-update) | async-done | bytes 812048 | tf_op jit(solution)/shard_map/psum | solution.py:147
  (140 shorter events, 45.3 us)
Async XLA Ops:
  7.2 7.2 %copy-start = (bf16[1024,1024]{1,0:T(8,128)(2,1)S(1)}, bf16[1024,1024]{1,0:T(8,128)(2,1)}, u32[]{:S(2)}) copy-start(bf16[1024,1024]{1,0:T(8,128)(2,1)} %param.13) | copy-start | bytes 6291460
  7.2 13.3 %copy-start.23 = (bf16[1,32,1024]{2,1,0:T(8,128)(2,1)S(1)}, bf16[1,32,1024]{2,1,0:T(8,128)(2,1)}, u32[]{:S(2)}) copy-start(bf16[1,32,1024]{2,1,0:T(8,128)(2,1)} %param.8) | copy-start | bytes 196612
  7.2 279.5 %reduce-scatter.4.cloned.1.call-start = ((), (), s32[]{:S(2)}) async-start(), calls=%async_computation.2 | async-start | bytes 7372800
  7.2 10.5 %collective-permute-start.1 = (bf16[32,1024]{1,0:T(8,128)(2,1)}, bf16[32,1024]{1,0:T(8,128)(2,1)S(1)}, u32[]{:S(2)}, u32[]{:S(2)}) collective-permute-start(bf16[32,1024]{1,0:T(8,128)(2,1)} %bitcast.70), channel_id=1, source_target_pairs={{1,0},{2,1},{3,2},{4,3},{5,4},{6,5},{7,6},{0,7},{9,8},{10,9},{11,1... | collective-permute-start | bytes 196616 | tf_op jit(solution)/shard_map/ppermute | solution.py:21
  13.3 7.2 %collective-permute-start = (bf16[32,1024]{1,0:T(8,128)(2,1)}, bf16[32,1024]{1,0:T(8,128)(2,1)S(1)}, u32[]{:S(2)}, u32[]{:S(2)}) collective-permute-start(bf16[32,1024]{1,0:T(8,128)(2,1)} %bitcast.71), channel_id=1, source_target_pairs={{0,1},{1,2},{2,3},{3,4},{4,5},{5,6},{6,7},{7,0},{8,9},{9,10},{10,1... | collective-permute-start | bytes 196616 | tf_op jit(solution)/shard_map/ppermute | solution.py:19
  14.4 6.9 %copy-start.34 = (s32[768]{0:T(1024)}, s32[768]{0:T(1024)S(1)}, u32[]{:S(2)}) copy-start(s32[768]{0:T(1024)S(1)} %reshape.146) | copy-start | bytes 9220
  14.4 6.1 %copy-start.7 = (bf16[1024,2048]{1,0:T(8,128)(2,1)S(1)}, bf16[1024,2048]{1,0:T(8,128)(2,1)}, u32[]{:S(2)}) copy-start(bf16[1024,2048]{1,0:T(8,128)(2,1)} %param.14) | copy-start | bytes 12582916
  16.5 4.8 %copy-start.8 = (f32[256,1024]{0,1:T(8,128)}, f32[256,1024]{0,1:T(8,128)S(1)}, u32[]{:S(2)}) copy-start(f32[256,1024]{0,1:T(8,128)S(1)} %get-tuple-element.67) | copy-start | bytes 3145732
  16.5 4.8 %copy-start.27 = (f32[256,16]{0,1:T(8,128)}, f32[256,16]{0,1:T(8,128)S(1)}, u32[]{:S(2)}) copy-start(f32[256,16]{0,1:T(8,128)S(1)} %get-tuple-element.66) | copy-start | bytes 49156
  16.6 4.8 %copy-start.29 = (f32[256,16]{0,1:T(8,128)}, f32[256,16]{0,1:T(8,128)S(1)}, u32[]{:S(2)}) copy-start(f32[256,16]{0,1:T(8,128)S(1)} %fusion.18) | copy-start | bytes 49156
  52.4 16.9 %copy-start.21 = (f32[256,16,3]{0,1,2:T(8,128)}, f32[256,16,3]{0,1,2:T(8,128)S(1)}, u32[]{:S(2)}) copy-start(f32[256,16,3]{0,1,2:T(8,128)S(1)} %fusion.16) | copy-start | bytes 147460
  74.7 4.9 %copy-start.16 = (bf16[1024,100]{0,1:T(8,128)(2,1)S(1)}, bf16[1024,100]{0,1:T(8,128)(2,1)}, u32[]{:S(2)}) copy-start(bf16[1024,100]{0,1:T(8,128)(2,1)} %param.15) | copy-start | bytes 614404
  76.4 4.1 %copy-start.32 = (f32[256]{0:T(256)}, f32[256]{0:T(256)S(1)}, u32[]{:S(2)}) copy-start(f32[256]{0:T(256)S(1)} %broadcast_multiply_fusion.2) | copy-start | bytes 3076
  87.9 5.5 %copy-start.38 = (f32[256]{0:T(256)S(1)}, f32[256]{0:T(256)}, u32[]{:S(2)}) copy-start(f32[256]{0:T(256)} %copy-done.37) | copy-start | bytes 3076
  88.0 5.5 %copy-start.3 = (f32[256,1024]{1,0:T(8,128)S(1)}, f32[256,1024]{1,0:T(8,128)}, u32[]{:S(2)}) copy-start(f32[256,1024]{1,0:T(8,128)} %copy.28) | copy-start | bytes 3145732
  88.0 5.5 %copy-start.5 = (bf16[256,1024]{1,0:T(8,128)(2,1)S(1)}, bf16[256,1024]{1,0:T(8,128)(2,1)}, u32[]{:S(2)}) copy-start(bf16[256,1024]{1,0:T(8,128)(2,1)} %param.9) | copy-start | bytes 1572868
  88.0 5.5 %copy-start.33 = (f32[256]{0:T(256)S(1)}, f32[256]{0:T(256)}, u32[]{:S(2)}) copy-start(f32[256]{0:T(256)} %copy-done.32) | copy-start | bytes 3076
  88.0 5.5 %copy-start.36 = (f32[256]{0:T(256)S(1)}, f32[256]{0:T(256)}, u32[]{:S(2)}) copy-start(f32[256]{0:T(256)} %copy-done.35) | copy-start | bytes 3076
  116.3 27.9 %copy-start.6 = (bf16[256,1024]{1,0:T(8,128)(2,1)S(1)}, bf16[256,1024]{1,0:T(8,128)(2,1)}, u32[]{:S(2)}) copy-start(bf16[256,1024]{1,0:T(8,128)(2,1)} %param.9) | copy-start | bytes 1572868
  142.1 5.8 %collective-permute-start.2 = (bf16[32,2048]{1,0:T(8,128)(2,1)S(1)}, bf16[32,2048]{1,0:T(8,128)(2,1)S(1)}, u32[]{:S(2)}, u32[]{:S(2)}) collective-permute-start(bf16[32,2048]{1,0:T(8,128)(2,1)S(1)} %get-tuple-element.62), channel_id=1, source_target_pairs={{0,7},{1,0},{2,1},{3,2},{4,3},{5,4},{6,5},{7,6},{8,15},{9,8},{10,9... | collective-permute-start | bytes 393224 | tf_op jit(solution)/shard_map/ppermute | solution.py:30
  144.2 8.2 %collective-permute-start.3 = (bf16[32,2048]{1,0:T(8,128)(2,1)S(1)}, bf16[32,2048]{1,0:T(8,128)(2,1)S(1)}, u32[]{:S(2)}, u32[]{:S(2)}) collective-permute-start(bf16[32,2048]{1,0:T(8,128)(2,1)S(1)} %get-tuple-element.63), channel_id=1, source_target_pairs={{0,1},{1,2},{2,3},{3,4},{4,5},{5,6},{6,7},{7,0},{8,9},{9,10},{10,1... | collective-permute-start | bytes 393224 | tf_op jit(solution)/shard_map/ppermute | solution.py:30
  144.2 8.2 %copy-start.24 = (bf16[1,32,1024]{2,1,0:T(8,128)(2,1)S(1)}, bf16[1,32,1024]{2,1,0:T(8,128)(2,1)}, u32[]{:S(2)}) copy-start(bf16[1,32,1024]{2,1,0:T(8,128)(2,1)} %param.8) | copy-start | bytes 196612
  167.2 156.4 %all-reduce.4.cloned.1.call-start = ((), (), s32[]{:S(2)}) async-start(), calls=%async_computation.1 | async-start | bytes 1626112 | tf_op jit(solution)/shard_map/psum | solution.py:147
  309.7 19.7 %copy-start.1 = (bf16[1024,1024]{1,0:T(8,128)(2,1)S(1)}, bf16[1024,1024]{1,0:T(8,128)(2,1)}, u32[]{:S(2)}) copy-start(bf16[1024,1024]{1,0:T(8,128)(2,1)} %param.13) | copy-start | bytes 6291460
  (21 other events, 36.3 us)
Sparse Core Ops, SparseCore 0:
  167.3 119.3 reduce-scatter.3
  289.7 33.7 all-reduce.3
where the time goes:
time: 339 us; the launch traced here: 337 us
  waiting for transfers between devices  139 us (41%)
  local copies, waits for them, and re-layouts  92.3 us (27%)
  other arithmetic  42.9 us (13%)
  blocking collectives  26.5 us (8%)
  between operations  16.5 us (5%)
  matrix products  12.4 us (4%)
  starting transfers between devices  8.24 us (2%)
    unnamed x3, waiting for transfers between devices  119 us
    gather x4, local copies, waits for them, and re-layouts, attend(): picked = table[source]  28.9 us
    unnamed x83, local copies, waits for them, and re-layouts  20.8 us
    add_any x2, local copies, waits for them, and re-layouts, attend(): key_norm = normalize_heads(picked[..., :width])  20.4 us
    psum x1, blocking collectives, on_device(): loss = lax.psum(local_loss[None], 'shard') / divisor  20.2 us
    scatter-add x1, other arithmetic, attend(): picked = table[source]  14.9 us
    psum x1, waiting for transfers between devices, on_device(): total = lax.psum(portion, 'member').astype(jnp.float32)  9.48 us
    slice x2, local copies, waits for them, and re-layouts, attend(): key_norm = normalize_heads(picked[..., :width])  8.54 us
  transfers between devices with their start and end apart: 6, of which 5 were waited for; matrix products, arithmetic and copies ran while one was open for 3% of the time, Pallas kernels for 0%

commit v1 on v0

v1 whole, which is shorter than its diff:
```python
import functools

import jax
import jax.numpy as jnp
from jax import lax
from jax.experimental import pallas as pl
from jax.experimental.pallas import tpu as pltpu
from jax.sharding import PartitionSpec as P

HEADS = 16
LANES = 128
BF = jnp.bfloat16
F32 = jnp.float32
MESH = pl.DeviceIdType.MESH


def mm(a, b):
    return jnp.dot(a, b, preferred_element_type=F32)


def mm_nt(a, b):
    return lax.dot_general(a, b, (((1,), (1,)), ((), ())), preferred_element_type=F32)


def mm_tn(a, b):
    return lax.dot_general(a, b, (((0,), (0,)), ((), ())), preferred_element_type=F32)


def kernel(
    members, shards,
    latent, embed, source, area, target, w_query, w_keyval, w_head,
    loss_out, d_latent, grad_query, grad_keyval, grad_head,
    lat3, lat4, table, query, q_norm, q_rstd, k_norm, k_rstd, expo, recip, mixed, hidden, d_hid,
    wh, preds, preds_in, ph, ph_in, ph_fin, part, part_in,
    own_dt, halo, halo_in, ob, dt4, dqs, dqs_in, pq, yq, zq, zq_in, pk, yk, zk, zk_in, fq, fk, fq_in, fk_in,
    halo_sem, lat_sem, pred_sem, head_sem, loss_sem, hfin_sem, dth_sem, dtm_sem, dq_sem,
    y_sem, zq_sem, zk_sem, fq_sem, fk_sem,
):
    rows, width = embed.shape
    nodes = latent.shape[0]
    variables = target.shape[1]
    m = lax.axis_index("member")
    s = lax.axis_index("shard")
    size = width // HEADS
    pairs = width // LANES
    chunk = width // members
    per_chunk = chunk // LANES
    out_rows = width // shards
    outer = shards // 2
    a = s // 2
    b = lax.rem(s, 2)
    padded = lat3.shape[0]
    scale = (members * rows * shards) ** (-0.5)

    def send(src, dst, sems, index, to_m, to_s):
        return pltpu.make_async_remote_copy(
            src_ref=src, dst_ref=dst, send_sem=sems.at[0, index], recv_sem=sems.at[1, index],
            device_id=(to_m, to_s), device_id_type=MESH,
        )

    def member(i):
        return lax.rem(m + i, members)

    def shard(i):
        return lax.rem(s + i, shards)

    barrier = pltpu.get_barrier_semaphore()
    for i in range(1, members):
        pl.semaphore_signal(barrier, inc=1, device_id=(member(i), s), device_id_type=MESH)
    for i in range(1, shards):
        pl.semaphore_signal(barrier, inc=1, device_id=(m, shard(i)), device_id_type=MESH)
    pl.semaphore_wait(barrier, members + shards - 2)

    halo_up = send(latent, lat3.at[pl.ds(0, nodes)], halo_sem, 0, m, shard(1))
    halo_down = send(latent, lat3.at[pl.ds(2 * nodes, nodes)], halo_sem, 1, m, shard(shards - 1))
    halo_up.start()
    halo_down.start()
    lat_copies = [
        send(latent, lat4.at[pl.ds(i * nodes, nodes)], lat_sem, i, member(i), s) for i in range(1, members)
    ]
    for copy in lat_copies:
        copy.start()
    lat3[nodes : 2 * nodes, :] = latent[...]
    lat3[3 * nodes :, :] = jnp.zeros((padded - 3 * nodes, width), BF)
    lat4[:nodes, :] = latent[...]

    wh[...] = jnp.zeros(wh.shape, BF)
    wh[:, :variables] = w_head[...]

    def query_step(i, carry):
        cols = pl.ds(pl.multiple_of(i * 256, 256), 256)
        query[:, cols] = mm(embed[...], w_query[:, cols])
        return carry

    lax.fori_loop(0, width // 256, query_step, 0)

    lane = lax.broadcasted_iota(jnp.int32, (1, LANES), 1)
    masks = [(lane // size == h).astype(F32) for h in range(2)]
    row_head = lax.broadcasted_iota(jnp.int32, (LANES, LANES), 0) // size
    col_head = lax.broadcasted_iota(jnp.int32, (LANES, LANES), 1) // size
    same = jnp.where(row_head == col_head, 1.0 / size, 0.0).astype(BF)

    def head_mean(x):
        return mm(x.astype(BF), same)

    def stacked(x):
        return jnp.concatenate([x * masks[0], x * masks[1]], axis=0).astype(BF)

    def unstacked(x):
        return x[:padded] * masks[0] + x[padded:] * masks[1]

    ones = jnp.ones((padded, LANES), F32)
    in_head = stacked(ones)
    src = source[...] - (s - 1) * nodes
    src = jnp.where(src < 0, src + shards * nodes, src)
    src = jnp.where(src >= shards * nodes, src - shards * nodes, src)
    node = lax.broadcasted_iota(jnp.int32, (rows, padded), 1)
    count = jnp.zeros((rows, padded), F32)
    for k in range(source.shape[1]):
        count = count + (src[:, k : k + 1] == node).astype(F32)
    count2 = jnp.concatenate([count, count], axis=1)

    halo_up.wait()
    halo_down.wait()

    def table_step(i, carry):
        cols = pl.ds(pl.multiple_of(i * 256, 256), 256)
        table[:, cols] = mm(lat3[...], w_keyval[:, cols]).astype(BF)
        return carry

    lax.fori_loop(0, 2 * width // 256, table_step, 0)

    for p in range(pairs):
        cols = slice(p * LANES, (p + 1) * LANES)
        q = query[:, cols]
        r = lax.rsqrt(head_mean(q * q) + 1e-06)
        qn = (q * r).astype(BF)
        q_norm[:, cols] = qn
        q_rstd[:, cols] = r
        key = table[:, cols].astype(F32)
        rk = lax.rsqrt(head_mean(key * key) + 1e-06)
        kn = key * rk
        k_norm[:, cols] = kn
        k_rstd[:, cols] = rk
        score = mm_nt(qn, stacked(kn))
        e = (count2 * jnp.exp(score * size ** (-0.5))).astype(BF)
        expo[p] = e
        v2 = stacked(table[:, width + p * LANES : width + (p + 1) * LANES].astype(F32))
        both = mm(e, jnp.concatenate([v2, in_head], axis=1))
        inv = 1.0 / both[:, LANES:]
        out = both[:, :LANES] * inv
        recip[:, cols] = inv
        mixed[:, cols] = out
        hidden[:, cols] = embed[:, cols].astype(F32) + out

    hid = hidden[...]
    center = hid - jnp.mean(hid, -1, keepdims=True)
    rstd = lax.rsqrt(jnp.mean(center * center, -1, keepdims=True) + 1e-05)
    nhat = center * rstd
    hidden[...] = nhat
    normed = nhat.astype(BF)
    pred = mm(normed, wh[...])
    preds[...] = pred.astype(BF)
    pred_copies = [send(preds, preds_in.at[i], pred_sem, i, member(i), s) for i in range(1, members)]
    for copy in pred_copies:
        copy.start()
    valid = (lane < variables).astype(F32)
    weights = area[...]
    want = jnp.concatenate([target[...], jnp.zeros((rows, LANES - variables), F32)], axis=1)
    miss = pred - want
    miss_sq = miss * miss + 0.0625
    miss_inv = lax.rsqrt(miss_sq)
    pair_value = jnp.zeros((rows, LANES), F32)
    pair_slope = jnp.zeros((rows, LANES), F32)
    for i in range(1, members):
        pred_copies[i - 1].wait()
        delta = pred - preds_in[i].astype(F32)
        square = delta * delta + 0.0625
        inv = lax.rsqrt(square)
        pair_value = pair_value + square * inv
        pair_slope = pair_slope + delta * inv
    pair_scale = 1.0 / (members * (members - 1))
    share = weights * valid * (miss_sq * miss_inv / members - 0.5 * pair_scale * pair_value)
    part[...] = jnp.broadcast_to(jnp.sum(share, 0, keepdims=True), part.shape)
    loss_copies = [send(part, part_in.at[i], loss_sem, i, m, shard(i)) for i in range(1, shards)]
    for copy in loss_copies:
        copy.start()
    d_outb = (weights * (miss * miss_inv / members - pair_scale * pair_slope)).astype(BF)
    per_block = 256 // out_rows
    head_part = mm_tn(normed, d_outb) * scale
    for j in range(shards):
        ph[j] = head_part[j * out_rows : (j + 1) * out_rows].astype(BF)
    head_copies = [
        send(ph.at[shard(i)], ph_in.at[i], head_sem, i, m, shard(i)) for i in range(1, shards)
    ]
    for copy in head_copies:
        copy.start()
    d_normed = mm_nt(d_outb, wh[...])
    nhat = hidden[...]
    d_hid[...] = rstd * (
        d_normed
        - jnp.mean(d_normed, -1, keepdims=True)
        - nhat * jnp.mean(d_normed * nhat, -1, keepdims=True)
    )

    def dq_copy(c):
        slot = lax.rem(c - m + members, members)
        return send(dqs.at[c], dqs_in.at[slot], dq_sem, slot, c, s)

    def halo_copies(c):
        return [
            send(halo.at[0, c], halo_in.at[0, c], dth_sem, 2 * c, m, shard(shards - 1)),
            send(halo.at[1, c], halo_in.at[1, c], dth_sem, 2 * c + 1, m, shard(1)),
        ]

    for c in range(members):
        for t in range(per_chunk):
            p = c * per_chunk + t
            cols = slice(p * LANES, (p + 1) * LANES)
            here = slice(t * LANES, (t + 1) * LANES)
            there = slice(chunk + t * LANES, chunk + (t + 1) * LANES)
            d_out = d_hid[:, cols] * recip[:, cols]
            d_outl = d_out.astype(BF)
            kn = k_norm[:, cols]
            k2 = stacked(kn)
            v2 = stacked(table[:, width + p * LANES : width + (p + 1) * LANES].astype(F32))
            left = jnp.concatenate([d_outl, (d_out * mixed[:, cols]).astype(BF)], axis=1)
            d_weight = mm_nt(left, jnp.concatenate([v2, -in_head], axis=1))
            e = expo[p]
            d_score = (e.astype(F32) * d_weight * size ** (-0.5)).astype(BF)
            qn = q_norm[:, cols]
            d_qn = mm(d_score, k2)
            qf = qn.astype(F32)
            dqs[c, :, here] = (q_rstd[:, cols] * (d_qn - qf * head_mean(d_qn * qf))).astype(BF)
            d_kn = unstacked(mm_tn(d_score, qn))
            d_key = k_rstd[:, cols] * (d_kn - kn * head_mean(d_kn * kn))
            d_val = unstacked(mm_tn(e, d_outl))
            for where, grad in ((here, d_key), (there, d_val)):
                halo[0, c, :, where] = grad[:nodes].astype(BF)
                own_dt[c, :, where] = grad[nodes : 2 * nodes]
                halo[1, c, :, where] = grad[2 * nodes : 3 * nodes].astype(BF)
        for copy in halo_copies(c):
            copy.start()

        @pl.when(c != m)
        def _():
            dq_copy(c).start()

    total = part[...]
    for i in range(1, shards):
        loss_copies[i - 1].wait()
        total = total + part_in[i]
    loss_out[...] = jnp.broadcast_to(
        jnp.sum(total[0:1], -1, keepdims=True) / (rows * shards * variables), loss_out.shape
    )
    head_sum = ph[s].astype(F32)
    for i in range(1, shards):
        head_copies[i - 1].wait()
        head_sum = head_sum + ph_in[i].astype(F32)
    ph_fin[m] = head_sum.astype(BF)
    for i in range(1, members):
        pltpu.make_async_remote_copy(
            src_ref=ph_fin.at[m], dst_ref=ph_fin.at[m], send_sem=hfin_sem.at[0, i],
            recv_sem=hfin_sem.at[1, i], device_id=(member(i), s), device_id_type=MESH,
        ).start()

    for c in range(members):
        for copy in halo_copies(c):
            copy.wait()
        ob[c] = (own_dt[c] + halo_in[0, c].astype(F32) + halo_in[1, c].astype(F32)).astype(BF)

        @pl.when(c != m)
        def _():
            slot = lax.rem(c - m + members, members)
            send(ob.at[c], dt4.at[slot], dtm_sem, slot, c, s).start()

    dq_sum = dqs[m].astype(F32)
    for i in range(1, members):
        send(dqs.at[member(i)], dqs_in.at[i], dq_sem, i, member(i), s).wait()
        dq_sum = dq_sum + dqs_in[i].astype(F32)
    dq_sumb = dq_sum.astype(BF)
    for block in range(width // 256):
        piece = mm_tn(embed[:, block * 256 : (block + 1) * 256], dq_sumb) * scale
        for t in range(per_block):
            j = block * per_block + t
            pq[j % 2, j // 2] = piece[t * out_rows : (t + 1) * out_rows].astype(BF)
    partner = s + 1 - 2 * b
    y_query = send(pq.at[1 - b], yq, y_sem, 0, m, partner)
    y_query.start()

    dt4[0] = ob[m]
    for i in range(1, members):
        lat_copies[i - 1].wait()
        send(ob.at[member(i)], dt4.at[i], dtm_sem, i, member(i), s).wait()
    right = dt4[...].reshape(members * nodes, 2 * chunk)
    for block in range(width // 256):
        piece = mm_tn(lat4[:, block * 256 : (block + 1) * 256], right) * scale
        for t in range(per_block):
            j = block * per_block + t
            pk[j % 2, j // 2] = piece[t * out_rows : (t + 1) * out_rows].astype(BF)
    y_keyval = send(pk.at[1 - b], yk, y_sem, 1, m, partner)
    y_keyval.start()

    d_lat = jnp.zeros((nodes, width), F32)
    for c in range(members):
        d_lat = d_lat + mm_nt(ob[c, :, :chunk], w_keyval[:, c * chunk : (c + 1) * chunk])
        d_lat = d_lat + mm_nt(ob[c, :, chunk:], w_keyval[:, width + c * chunk : width + (c + 1) * chunk])
    d_latent[...] = d_lat

    def other(i):
        return lax.rem(a + i, outer)

    def z_copies(from_ref, in_ref, sems):
        return [
            send(from_ref.at[other(i)], in_ref.at[i], sems, i, m, 2 * other(i) + b)
            for i in range(1, outer)
        ]

    y_query.wait()
    zq[...] = (pq[b].astype(F32) + yq[...].astype(F32)).astype(BF)
    zq_copies = z_copies(zq, zq_in, zq_sem)
    for copy in zq_copies:
        copy.start()
    y_keyval.wait()
    zk[...] = (pk[b].astype(F32) + yk[...].astype(F32)).astype(BF)
    zk_copies = z_copies(zk, zk_in, zk_sem)
    for copy in zk_copies:
        copy.start()

    done = zq[a].astype(F32)
    for i in range(1, outer):
        zq_copies[i - 1].wait()
        done = done + zq_in[i].astype(F32)
    fq[...] = done.astype(BF)
    fq_copies = [send(fq, fq_in.at[i], fq_sem, i, member(i), s) for i in range(1, members)]
    for copy in fq_copies:
        copy.start()
    done = zk[a].astype(F32)
    for i in range(1, outer):
        zk_copies[i - 1].wait()
        done = done + zk_in[i].astype(F32)
    fk[...] = done.astype(BF)
    fk_copies = [send(fk, fk_in.at[i], fk_sem, i, member(i), s) for i in range(1, members)]
    for copy in fk_copies:
        copy.start()

    for i in range(1, members):
        pltpu.make_async_remote_copy(
            src_ref=ph_fin.at[m], dst_ref=ph_fin.at[member(members - i)], send_sem=hfin_sem.at[0, i],
            recv_sem=hfin_sem.at[1, i], device_id=(member(i), s), device_id_type=MESH,
        ).wait()
    head_total = ph_fin[0].astype(F32)
    for c in range(1, members):
        head_total = head_total + ph_fin[c].astype(F32)
    grad_head[...] = head_total[:, :variables]

    def at(start, i):
        return pl.ds(pl.multiple_of(start + member(members - i) * chunk, LANES), chunk)

    grad_query[:, at(0, 0)] = fq[...].astype(F32)
    for i in range(1, members):
        fq_copies[i - 1].wait()
        grad_query[:, at(0, i)] = fq_in[i].astype(F32)
    for i in range(members):
        if i:
            fk_copies[i - 1].wait()
        block = fk_in[i].astype(F32) if i else fk[...].astype(F32)
        grad_keyval[:, at(0, i)] = block[:, :chunk]
        grad_keyval[:, at(width, i)] = block[:, chunk:]


def on_device(latent, grid_embed, edge_src, area, target, w_query, w_keyval, w_head):
    rows, width = grid_embed.shape
    nodes = latent.shape[1]
    shards = lax.axis_size("shard")
    members = lax.axis_size("member")
    variables = target.shape[1]
    out_rows = width // shards
    chunk = width // members
    outer = shards // 2
    pairs = width // LANES
    padded = -(-3 * nodes // LANES) * LANES
    vm = pltpu.VMEM
    dma = lambda n: pltpu.SemaphoreType.DMA((2, n))
    outs = (
        jax.ShapeDtypeStruct((8, LANES), F32),
        jax.ShapeDtypeStruct((nodes, width), F32),
        jax.ShapeDtypeStruct((out_rows, width), F32),
        jax.ShapeDtypeStruct((out_rows, 2 * width), F32),
        jax.ShapeDtypeStruct((out_rows, variables), F32),
    )
    scratch = [
        vm((padded, width), BF),
        vm((members * nodes, width), BF),
        vm((padded, 2 * width), BF),
        vm((rows, width), F32),
        vm((rows, width), BF),
        vm((rows, width), F32),
        vm((padded, width), F32),
        vm((padded, width), F32),
        vm((pairs, rows, 2 * padded), BF),
        vm((rows, width), F32),
        vm((rows, width), F32),
        vm((rows, width), F32),
        vm((rows, width), F32),
        vm((width, LANES), BF),
        vm((rows, LANES), BF),
        vm((members, rows, LANES), BF),
        vm((shards, out_rows, LANES), BF),
        vm((shards, out_rows, LANES), BF),
        vm((members, out_rows, LANES), BF),
        vm((8, LANES), F32),
        vm((shards, 8, LANES), F32),
        vm((members, nodes, 2 * chunk), F32),
        vm((2, members, nodes, 2 * chunk), BF),
        vm((2, members, nodes, 2 * chunk), BF),
        vm((members, nodes, 2 * chunk), BF),
        vm((members, nodes, 2 * chunk), BF),
        vm((members, rows, chunk), BF),
        vm((members, rows, chunk), BF),
        vm((2, outer, out_rows, chunk), BF),
        vm((outer, out_rows, chunk), BF),
        vm((outer, out_rows, chunk), BF),
        vm((outer, out_rows, chunk), BF),
        vm((2, outer, out_rows, 2 * chunk), BF),
        vm((outer, out_rows, 2 * chunk), BF),
        vm((outer, out_rows, 2 * chunk), BF),
        vm((outer, out_rows, 2 * chunk), BF),
        vm((out_rows, chunk), BF),
        vm((out_rows, 2 * chunk), BF),
        vm((members, out_rows, chunk), BF),
        vm((members, out_rows, 2 * chunk), BF),
        dma(2), dma(members), dma(members), dma(shards), dma(shards), dma(members),
        dma(2 * members), dma(members), dma(members),
        dma(2), dma(outer), dma(outer), dma(members), dma(members),
    ]
    spec = pl.BlockSpec(memory_space=pltpu.VMEM)
    loss, d_lat, grad_q, grad_kv, grad_h = pl.pallas_call(
        functools.partial(kernel, members, shards),
        out_shape=outs,
        in_specs=[spec] * 8,
        out_specs=tuple([spec] * 5),
        scratch_shapes=scratch,
        compiler_params=pltpu.CompilerParams(
            collective_id=0, has_side_effects=True, vmem_limit_bytes=52 * 1024 * 1024
        ),
    )(latent[0], grid_embed, edge_src, area[:, None], target, w_query, w_keyval, w_head)
    return loss[0, :1], d_lat[None], grad_q, grad_kv, grad_h


def solution(mesh):
    placed = (
        P("member", "shard", None),
        P("shard", None),
        P("shard", None),
        P("shard"),
        P("shard", None),
        P(),
        P(),
        P(),
    )
    return jax.shard_map(
        on_device,
        mesh=mesh,
        in_specs=placed,
        out_specs=(
            P("member"),
            P("member", "shard", None),
            P("shard", None),
            P("shard", None),
            P("shard", None),
        ),
        check_vma=False,
    )
```

time: 339 us -> 85.6 us (0.25)
  the two profiles are of different devices: /device:TPU:0 before, /device:TPU:9 now
where the time goes in v1:
time: 85.6 us; the launch traced here: 85.3 us
  Pallas kernels  74 us (86%)
  local copies, waits for them, and re-layouts  10.6 us (12%)
    pallas_call x1, Pallas kernels, on_device(): pl.pallas_call(functools.partial(kernel, members, shards), out_shape=outs...  74 us
    unnamed x11, local copies, waits for them, and re-layouts  9.26 us

profile of v1, /device:TPU:9, one launch (start us, length us, event | category | flops | bytes accessed | tf_op | source)
XLA Modules:
  0.0 85.3 jit_solution(15605594462258133866)
XLA Ops:
  0.6 0.8 copy.17.source
  1.5 0.8 copy.18.area
  2.3 1.0 %copy.19.target = f32[256,100]{1,0:T(8,128)S(1)} copy(f32[256,100]{0,1:T(8,128)} %param.12) | data formatting | bytes 204800 | tf_op args[4]
  3.3 1.1 %copy.20.w_head = bf16[1024,100]{1,0:T(8,128)(2,1)S(1)} copy(bf16[1024,100]{0,1:T(8,128)(2,1)} %param.15) | data formatting | bytes 409600 | tf_op args[7]
  4.4 0.0 copy-start
  4.4 1.0 %copy-done = bf16[256,1024]{1,0:T(8,128)(2,1)S(1)} copy-done((bf16[256,1024]{1,0:T(8,128)(2,1)S(1)}, bf16[256,1024]{1,0:T(8,128)(2,1)}, u32[]{:S(2)}) %copy-start) | copy-done | bytes 524312
  5.4 0.0 copy-start.1
  5.4 0.8 copy-done.1
  6.3 74.0 %shard_map.119 = (f32[8,128]{1,0:T(8,128)S(1)}, f32[32,1024]{1,0:T(8,128)S(1)}, f32[128,1024]{1,0:T(8,128)S(1)}, f32[128,2048]{1,0:T(8,128)}, f32[128,100]{1,0:T(8,128)S(1)}) custom-call(bf16[32,1024]{1,0:T(8,128)(2,1)S(1)} %bitcast.5, bf16[256,1024]{1,0:T(8,128)(2,1)S(1)} %copy-done, s32[256,3]{1,0:T(8,128)S(1)} %copy.17.source, f32[256,1]{1,0:T(8,128)S(1)} %copy.18.area, ...), custom_call_target="tpu_custom_call" | custom-call | tf_op jit(solution)/shard_map/pallas_call | solution.py:438
  80.3 0.5 slice.3
  80.8 0.7 copy.21
  81.5 0.7 copy.25
  82.2 0.8 copy.26
  83.0 2.3 %copy.27 = f32[128,2048]{1,0:T(8,128)} copy(f32[128,2048]{1,0:T(8,128)} %get-tuple-element.33) | data formatting | bytes 2097152
Async XLA Ops:
  4.4 1.0 %copy-start = (bf16[256,1024]{1,0:T(8,128)(2,1)S(1)}, bf16[256,1024]{1,0:T(8,128)(2,1)}, u32[]{:S(2)}) copy-start(bf16[256,1024]{1,0:T(8,128)(2,1)} %embed.1) | copy-start | bytes 1572868
  5.4 0.8 copy-start.1

commit v2 on v1

--- a/solution.py
+++ b/solution.py
@@ -28,17 +28,26 @@
 
 def kernel(
     members, shards,
-    latent, embed, source, area, target, w_query, w_keyval, w_head,
+    latent_hbm, embed_hbm, source, area, target, w_query_hbm, w_keyval_hbm, w_head,
     loss_out, d_latent, grad_query, grad_keyval, grad_head,
-    lat3, lat4, table, query, q_norm, q_rstd, k_norm, k_rstd, expo, recip, mixed, hidden, d_hid,
+    latent, embed, w_query, w_keyval, meta,
+    lat3, lat4, lat_t, lat_z, table, query, q_norm, q_rstd, k_norm, k_rstd, expo, recip, mixed, hidden, d_hid,
     wh, preds, preds_in, ph, ph_in, ph_fin, part, part_in,
-    own_dt, halo, halo_in, ob, dt4, dqs, dqs_in, pq, yq, zq, zq_in, pk, yk, zk, zk_in, fq, fk, fq_in, fk_in,
+    own_dt, halo, halo_in, ob, dt4, dqs, dqs_in, pq, yq, zq, zq_in, dtz, pk, yk, fq, fk,
     halo_sem, lat_sem, pred_sem, head_sem, loss_sem, hfin_sem, dth_sem, dtm_sem, dq_sem,
-    y_sem, zq_sem, zk_sem, fq_sem, fk_sem,
+    y_sem, zq_sem, latz_sem, up_sem, down_sem, fq_sem, fk_sem, load_sem,
 ):
+    loads = [
+        pltpu.make_async_copy(src, dst, load_sem.at[i])
+        for i, (src, dst) in enumerate(
+            ((latent_hbm, latent), (embed_hbm, embed), (w_query_hbm, w_query), (w_keyval_hbm, w_keyval))
+        )
+    ]
+    for load in loads:
+        load.start()
     rows, width = embed.shape
     nodes = latent.shape[0]
-    variables = target.shape[1]
+    variables = target.shape[0]
     m = lax.axis_index("member")
     s = lax.axis_index("shard")
     size = width // HEADS
@@ -71,6 +80,7 @@
         pl.semaphore_signal(barrier, inc=1, device_id=(m, shard(i)), device_id_type=MESH)
     pl.semaphore_wait(barrier, members + shards - 2)
 
+    loads[0].wait()
     halo_up = send(latent, lat3.at[pl.ds(0, nodes)], halo_sem, 0, m, shard(1))
     halo_down = send(latent, lat3.at[pl.ds(2 * nodes, nodes)], halo_sem, 1, m, shard(shards - 1))
     halo_up.start()
@@ -85,7 +95,13 @@
     lat4[:nodes, :] = latent[...]
 
     wh[...] = jnp.zeros(wh.shape, BF)
-    wh[:, :variables] = w_head[...]
+    wh[:variables, :] = w_head[...]
+    meta[...] = jnp.zeros(meta.shape, F32)
+    meta[:variables, :] = target[...]
+    meta[104:105, :] = area[...]
+    meta[112 : 112 + source.shape[0], :] = source[...].astype(F32)
+    loads[1].wait()
+    loads[2].wait()
 
     def query_step(i, carry):
         cols = pl.ds(pl.multiple_of(i * 256, 256), 256)
@@ -111,17 +127,19 @@
 
     ones = jnp.ones((padded, LANES), F32)
     in_head = stacked(ones)
-    src = source[...] - (s - 1) * nodes
+    turned = meta[...].T
+    src = turned - ((s - 1) * nodes).astype(F32)
     src = jnp.where(src < 0, src + shards * nodes, src)
     src = jnp.where(src >= shards * nodes, src - shards * nodes, src)
-    node = lax.broadcasted_iota(jnp.int32, (rows, padded), 1)
+    node = lax.broadcasted_iota(jnp.int32, (rows, padded), 1).astype(F32)
     count = jnp.zeros((rows, padded), F32)
-    for k in range(source.shape[1]):
-        count = count + (src[:, k : k + 1] == node).astype(F32)
+    for k in range(source.shape[0]):
+        count = count + (src[:, 112 + k : 113 + k] == node).astype(F32)
     count2 = jnp.concatenate([count, count], axis=1)
 
     halo_up.wait()
     halo_down.wait()
+    loads[3].wait()
 
     def table_step(i, carry):
         cols = pl.ds(pl.multiple_of(i * 256, 256), 256)
@@ -129,6 +147,27 @@
         return carry
 
     lax.fori_loop(0, 2 * width // 256, table_step, 0)
+
+    for copy in lat_copies:
+        copy.wait()
+    held = members * nodes
+    eye = lax.broadcasted_iota(jnp.int32, (held, held), 0) == lax.broadcasted_iota(jnp.int32, (held, held), 1)
+    eye = eye.astype(F32).astype(BF)
+    two = 2 * out_rows
+    for block in range(width // 256):
+        piece = mm_tn(lat4[:, block * 256 : (block + 1) * 256], eye).astype(BF)
+        for t in range(256 // two):
+            lat_t[block * (256 // two) + t] = piece[t * two : (t + 1) * two]
+
+    def other(i):
+        return lax.rem(a + i, outer)
+
+    latz_copies = [
+        send(lat_t.at[other(i)], lat_z.at[a], latz_sem, i, m, 2 * other(i) + b) for i in range(1, outer)
+    ]
+    for copy in latz_copies:
+        copy.start()
+    lat_z[a] = lat_t[a]
 
     for p in range(pairs):
         cols = slice(p * LANES, (p + 1) * LANES)
@@ -159,14 +198,14 @@
     nhat = center * rstd
     hidden[...] = nhat
     normed = nhat.astype(BF)
-    pred = mm(normed, wh[...])
+    pred = mm_nt(normed, wh[...])
     preds[...] = pred.astype(BF)
     pred_copies = [send(preds, preds_in.at[i], pred_sem, i, member(i), s) for i in range(1, members)]
     for copy in pred_copies:
         copy.start()
     valid = (lane < variables).astype(F32)
-    weights = area[...]
-    want = jnp.concatenate([target[...], jnp.zeros((rows, LANES - variables), F32)], axis=1)
+    weights = turned[:, 104:105]
+    want = turned * valid
     miss = pred - want
     miss_sq = miss * miss + 0.0625
     miss_inv = lax.rsqrt(miss_sq)
@@ -195,7 +234,7 @@
     ]
     for copy in head_copies:
         copy.start()
-    d_normed = mm_nt(d_outb, wh[...])
+    d_normed = mm(d_outb, wh[...])
     nhat = hidden[...]
     d_hid[...] = rstd * (
         d_normed
@@ -250,9 +289,7 @@
     for i in range(1, shards):
         loss_copies[i - 1].wait()
         total = total + part_in[i]
-    loss_out[...] = jnp.broadcast_to(
-        jnp.sum(total[0:1], -1, keepdims=True) / (rows * shards * variables), loss_out.shape
-    )
+    loss_out[...] = jnp.sum(total[0:1], -1, keepdims=True) / (rows * shards * variables)
     head_sum = ph[s].astype(F32)
     for i in range(1, shards):
         head_copies[i - 1].wait()
@@ -290,16 +327,22 @@
 
     dt4[0] = ob[m]
     for i in range(1, members):
-        lat_copies[i - 1].wait()
         send(ob.at[member(i)], dt4.at[i], dtm_sem, i, member(i), s).wait()
-    right = dt4[...].reshape(members * nodes, 2 * chunk)
-    for block in range(width // 256):
-        piece = mm_tn(lat4[:, block * 256 : (block + 1) * 256], right) * scale
-        for t in range(per_block):
-            j = block * per_block + t
-            pk[j % 2, j // 2] = piece[t * out_rows : (t + 1) * out_rows].astype(BF)
-    y_keyval = send(pk.at[1 - b], yk, y_sem, 1, m, partner)
-    y_keyval.start()
+    dtz[a] = dt4[...].reshape(held, 2 * chunk)
+
+    def upward(slot):
+        return send(dtz.at[slot], dtz.at[slot], up_sem, slot, m, 2 * (a + 1) + b)
+
+    def downward(slot):
+        return send(dtz.at[slot], dtz.at[slot], down_sem, slot, m, 2 * (a - 1) + b)
+
+    @pl.when(a < outer - 1)
+    def _():
+        upward(a).start()
+
+    @pl.when(a > 0)
+    def _():
+        downward(a).start()
 
     d_lat = jnp.zeros((nodes, width), F32)
     for c in range(members):
@@ -307,42 +350,72 @@
         d_lat = d_lat + mm_nt(ob[c, :, chunk:], w_keyval[:, width + c * chunk : width + (c + 1) * chunk])
     d_latent[...] = d_lat
 
-    def other(i):
-        return lax.rem(a + i, outer)
-
-    def z_copies(from_ref, in_ref, sems):
-        return [
-            send(from_ref.at[other(i)], in_ref.at[i], sems, i, m, 2 * other(i) + b)
-            for i in range(1, outer)
-        ]
-
-    y_query.wait()
-    zq[...] = (pq[b].astype(F32) + yq[...].astype(F32)).astype(BF)
-    zq_copies = z_copies(zq, zq_in, zq_sem)
-    for copy in zq_copies:
-        copy.start()
-    y_keyval.wait()
-    zk[...] = (pk[b].astype(F32) + yk[...].astype(F32)).astype(BF)
-    zk_copies = z_copies(zk, zk_in, zk_sem)
-    for copy in zk_copies:
-        copy.start()
+    zq_copies = [
+        send(zq.at[other(i)], zq_in.at[i], zq_sem, i, m, 2 * other(i) + b) for i in range(1, outer)
+    ]
+    for step in range(1, outer):
+
+        @pl.when(a - step >= 0)
+        def _():
+            upward(a - step).wait_recv()
+
+            @pl.when(a < outer - 1)
+            def _():
+                upward(a - step).start()
+
+        @pl.when(a + step < outer)
+        def _():
+            downward(a + step).wait_recv()
+
+            @pl.when(a > 0)
+            def _():
+                downward(a + step).start()
+
+        if step == 1:
+            y_query.wait()
+            zq[...] = (pq[b].astype(F32) + yq[...].astype(F32)).astype(BF)
+            for copy in zq_copies:
+                copy.start()
+
+    for copy in latz_copies:
+        copy.wait()
+    acc = jnp.zeros((two, 2 * chunk), F32)
+    for t in range(outer):
+        acc = acc + mm(lat_z[t], dtz[t])
+    acc = acc * scale
+    pk[0] = acc[:out_rows]
+    pk[1] = acc[out_rows:]
+    fk[m] = pk[1 - b].astype(BF)
+    y_keyval = send(fk.at[m], yk, y_sem, 1, m, partner)
+    y_keyval.start()
+
+    core = lax.rem(m, 2)
+    mate = m + 1 - 2 * core
+    chips = members // 2
+
+    def chip(i):
+        return lax.rem(m + 2 * i, members)
+
+    def spread(buffer, sems):
+        out = [send(buffer.at[m], buffer.at[m], sems, i, chip(i), s) for i in range(1, chips)]
+        out.append(send(buffer.at[m], buffer.at[m], sems, chips, mate, s))
+        for copy in out:
+            copy.start()
+        return out
+
+    def forward(buffer, sems, i):
+        slot = chip(chips - i)
+        return send(buffer.at[slot], buffer.at[slot], sems, chips + i, mate, s)
 
     done = zq[a].astype(F32)
     for i in range(1, outer):
         zq_copies[i - 1].wait()
         done = done + zq_in[i].astype(F32)
-    fq[...] = done.astype(BF)
-    fq_copies = [send(fq, fq_in.at[i], fq_sem, i, member(i), s) for i in range(1, members)]
-    for copy in fq_copies:
-        copy.start()
-    done = zk[a].astype(F32)
-    for i in range(1, outer):
-        zk_copies[i - 1].wait()
-        done = done + zk_in[i].astype(F32)
-    fk[...] = done.astype(BF)
-    fk_copies = [send(fk, fk_in.at[i], fk_sem, i, member(i), s) for i in range(1, members)]
-    for copy in fk_copies:
-        copy.start()
+    fq[m] = done.astype(BF)
+    q_copies = spread(fq, fq_sem)
+    y_keyval.wait()
+    fk[m] = (pk[b] + yk[...].astype(F32)).astype(BF)
+    k_copies = spread(fk, fk_sem)
 
     for i in range(1, members):
         pltpu.make_async_remote_copy(
@@ -352,21 +425,30 @@
     head_total = ph_fin[0].astype(F32)
     for c in range(1, members):
         head_total = head_total + ph_fin[c].astype(F32)
-    grad_head[...] = head_total[:, :variables]
-
-    def at(start, i):
-        return pl.ds(pl.multiple_of(start + member(members - i) * chunk, LANES), chunk)
-
-    grad_query[:, at(0, 0)] = fq[...].astype(F32)
-    for i in range(1, members):
-        fq_copies[i - 1].wait()
-        grad_query[:, at(0, i)] = fq_in[i].astype(F32)
-    for i in range(members):
-        if i:
-            fk_copies[i - 1].wait()
-        block = fk_in[i].astype(F32) if i else fk[...].astype(F32)
-        grad_keyval[:, at(0, i)] = block[:, :chunk]
-        grad_keyval[:, at(width, i)] = block[:, chunk:]
+    grad_head[...] = head_total.T[:variables]
+
+    for buffer, sems, copies in ((fq, fq_sem, q_copies), (fk, fk_sem, k_copies)):
+        for i in range(1, chips):
+            copies[i - 1].wait()
+            forward(buffer, sems, i).start()
+    for buffer, sems, copies in ((fq, fq_sem, q_copies), (fk, fk_sem, k_copies)):
+        copies[-1].wait()
+        for i in range(1, chips):
+            forward(buffer, sems, i).wait()
+    for c in range(members):
+        grad_query[:, c * chunk : (c + 1) * chunk] = fq[c]
+        grad_keyval[:, c * chunk : (c + 1) * chunk] = fk[c, :, :chunk]
+        grad_keyval[:, width + c * chunk : width + (c + 1) * chunk] = fk[c, :, chunk:]
+
+    for slot in range(outer):
+
+        @pl.when((a < outer - 1) & (a >= slot))
+        def _():
+            upward(slot).wait_send()
+
+        @pl.when((a > 0) & (a <= slot))
+        def _():
+            downward(slot).wait_send()
 
 
 def on_device(latent, grid_embed, edge_src, area, target, w_query, w_keyval, w_head):
@@ -375,6 +457,7 @@
     shards = lax.axis_size("shard")
     members = lax.axis_size("member")
     variables = target.shape[1]
+    held = members * nodes
     out_rows = width // shards
     chunk = width // members
     outer = shards // 2
@@ -383,15 +466,22 @@
     vm = pltpu.VMEM
     dma = lambda n: pltpu.SemaphoreType.DMA((2, n))
     outs = (
-        jax.ShapeDtypeStruct((8, LANES), F32),
+        jax.ShapeDtypeStruct((1, 1), F32),
         jax.ShapeDtypeStruct((nodes, width), F32),
-        jax.ShapeDtypeStruct((out_rows, width), F32),
-        jax.ShapeDtypeStruct((out_rows, 2 * width), F32),
-        jax.ShapeDtypeStruct((out_rows, variables), F32),
+        jax.ShapeDtypeStruct((out_rows, width), BF),
+        jax.ShapeDtypeStruct((out_rows, 2 * width), BF),
+        jax.ShapeDtypeStruct((variables, out_rows), F32),
     )
     scratch = [
+        vm((nodes, width), BF),
+        vm((rows, width), BF),
+        vm((width, width), BF),
+        vm((width, 2 * width), BF),
+        vm((LANES, rows), F32),
         vm((padded, width), BF),
-        vm((members * nodes, width), BF),
+        vm((held, width), BF),
+        vm((outer, 2 * out_rows, held), BF),
+        vm((outer, 2 * out_rows, held), BF),
         vm((padded, 2 * width), BF),
         vm((rows, width), F32),
         vm((rows, width), BF),
@@ -403,7 +493,7 @@
         vm((rows, width), F32),
         vm((rows, width), F32),
         vm((rows, width), F32),
-        vm((width, LANES), BF),
+        vm((LANES, width), BF),
         vm((rows, LANES), BF),
         vm((members, rows, LANES), BF),
         vm((shards, out_rows, LANES), BF),
@@ -422,30 +512,29 @@
         vm((outer, out_rows, chunk), BF),
         vm((outer, out_rows, chunk), BF),
         vm((outer, out_rows, chunk), BF),
-        vm((2, outer, out_rows, 2 * chunk), BF),
-        vm((outer, out_rows, 2 * chunk), BF),
-        vm((outer, out_rows, 2 * chunk), BF),
-        vm((outer, out_rows, 2 * chunk), BF),
-        vm((out_rows, chunk), BF),
+        vm((outer, held, 2 * chunk), BF),
+        vm((2, out_rows, 2 * chunk), F32),
         vm((out_rows, 2 * chunk), BF),
         vm((members, out_rows, chunk), BF),
         vm((members, out_rows, 2 * chunk), BF),
         dma(2), dma(members), dma(members), dma(shards), dma(shards), dma(members),
         dma(2 * members), dma(members), dma(members),
-        dma(2), dma(outer), dma(outer), dma(members), dma(members),
+        dma(2), dma(outer), dma(outer), dma(outer), dma(outer), dma(members), dma(members),
+        pltpu.SemaphoreType.DMA((4,)),
     ]
     spec = pl.BlockSpec(memory_space=pltpu.VMEM)
+    hbm = pl.BlockSpec(memory_space=pl.ANY)
     loss, d_lat, grad_q, grad_kv, grad_h = pl.pallas_call(
         functools.partial(kernel, members, shards),
         out_shape=outs,
-        in_specs=[spec] * 8,
+        in_specs=[hbm, hbm, spec, spec, spec, hbm, hbm, spec],
         out_specs=tuple([spec] * 5),
         scratch_shapes=scratch,
         compiler_params=pltpu.CompilerParams(
             collective_id=0, has_side_effects=True, vmem_limit_bytes=52 * 1024 * 1024
         ),
-    )(latent[0], grid_embed, edge_src, area[:, None], target, w_query, w_keyval, w_head)
-    return loss[0, :1], d_lat[None], grad_q, grad_kv, grad_h
+    )(latent[0], grid_embed, edge_src.T, area[None], target.T, w_query, w_keyval, w_head.T)
+    return loss[0], d_lat[None], grad_q.astype(F32), grad_kv.astype(F32), grad_h.T
 
 
 def solution(mesh):

time: 85.6 us -> 74.8 us (0.87)
  the two profiles are of different devices: /device:TPU:9 before, /device:TPU:0 now
where the time goes in v2:
time: 74.8 us; the launch traced here: 74.4 us
  Pallas kernels  63.7 us (85%)
  local copies, waits for them, and re-layouts  6.34 us (8%)
  between operations  2.48 us (3%)
  other arithmetic  1.92 us (3%)
    pallas_call x1, Pallas kernels, on_device(): pl.pallas_call(functools.partial(kernel, members, shards), out_shape=outs...  63.7 us
    unnamed x14, local copies, waits for them, and re-layouts  6.34 us

profile of v2, /device:TPU:0, one launch (start us, length us, event | category | flops | bytes accessed | tf_op | source)
XLA Modules:
  0.0 74.4 jit_solution(264634619125638976)
XLA Ops:
  0.6 0.0 copy-start
  0.6 1.0 %copy-done = bf16[256,1024]{1,0:T(8,128)(2,1)S(1)} copy-done((bf16[256,1024]{1,0:T(8,128)(2,1)S(1)}, bf16[256,1024]{1,0:T(8,128)(2,1)}, u32[]{:S(2)}) %copy-start) | copy-done | bytes 524312
  1.7 0.0 copy-start.1
  1.7 0.9 %copy-done.1 = bf16[1024,100]{0,1:T(8,128)(2,1)S(1)} copy-done((bf16[1024,100]{0,1:T(8,128)(2,1)S(1)}, bf16[1024,100]{0,1:T(8,128)(2,1)}, u32[]{:S(2)}) %copy-start.1) | copy-done | bytes 204824
  2.6 0.0 copy-start.2
  2.6 0.9 %copy-done.2 = f32[256,100]{0,1:T(8,128)S(1)} copy-done((f32[256,100]{0,1:T(8,128)S(1)}, f32[256,100]{0,1:T(8,128)}, u32[]{:S(2)}) %copy-start.2) | copy-done | bytes 102424
  3.5 0.0 copy-start.3
  3.5 0.8 %copy-done.3 = bf16[1,32,1024]{2,1,0:T(8,128)(2,1)S(1)} copy-done((bf16[1,32,1024]{2,1,0:T(8,128)(2,1)S(1)}, bf16[1,32,1024]{2,1,0:T(8,128)(2,1)}, u32[]{:S(2)}) %copy-start.3) | copy-done | bytes 65560
  4.3 0.0 copy-start.4
  4.3 0.7 copy-done.4
  5.0 0.0 copy-start.5
  5.0 0.7 copy-done.5
  5.7 63.7 %shard_map.119 = (f32[1,1]{1,0:T(1,128)}, f32[32,1024]{1,0:T(8,128)S(1)}, bf16[128,1024]{1,0:T(8,128)(2,1)S(1)}, bf16[128,2048]{1,0:T(8,128)(2,1)S(1)}, f32[100,128]{1,0:T(8,128)S(1)}) custom-call(bf16[32,1024]{1,0:T(8,128)(2,1)S(1)} %bitcast.11, bf16[256,1024]{1,0:T(8,128)(2,1)S(1)} %copy-done, s32[3,256]{1,0:T(4,128)S(1)} %bitcast.13, ...), custom_call_target="tpu_custom_call" | custom-call | tf_op jit(solution)/shard_map/pallas_call | solution.py:527
  69.4 1.1 %convert_element_type.7 = f32[128,2048]{1,0:T(8,128)} convert(bf16[128,2048]{1,0:T(8,128)(2,1)S(1)} %get-tuple-element.13) | non-fusion elementwise | flops 262144 | bytes 1572864 | tf_op jit(solution)/shard_map/convert_element_type | solution.py:537
  70.5 0.8 %convert_element_type.6 = f32[128,1024]{1,0:T(8,128)} convert(bf16[128,1024]{1,0:T(8,128)(2,1)S(1)} %get-tuple-element.12) | non-fusion elementwise | flops 131072 | bytes 786432 | tf_op jit(solution)/shard_map/convert_element_type | solution.py:537
  72.0 0.7 copy.17
  72.7 0.6 copy.18
Async XLA Ops:
  0.6 1.0 %copy-start = (bf16[256,1024]{1,0:T(8,128)(2,1)S(1)}, bf16[256,1024]{1,0:T(8,128)(2,1)}, u32[]{:S(2)}) copy-start(bf16[256,1024]{1,0:T(8,128)(2,1)} %embed_hbm.1) | copy-start | bytes 1572868
  1.7 0.9 %copy-start.1 = (bf16[1024,100]{0,1:T(8,128)(2,1)S(1)}, bf16[1024,100]{0,1:T(8,128)(2,1)}, u32[]{:S(2)}) copy-start(bf16[1024,100]{0,1:T(8,128)(2,1)} %param.15) | copy-start | bytes 614404
  2.6 0.9 %copy-start.2 = (f32[256,100]{0,1:T(8,128)S(1)}, f32[256,100]{0,1:T(8,128)}, u32[]{:S(2)}) copy-start(f32[256,100]{0,1:T(8,128)} %param.12) | copy-start | bytes 307204
  3.5 0.8 %copy-start.3 = (bf16[1,32,1024]{2,1,0:T(8,128)(2,1)S(1)}, bf16[1,32,1024]{2,1,0:T(8,128)(2,1)}, u32[]{:S(2)}) copy-start(bf16[1,32,1024]{2,1,0:T(8,128)(2,1)} %param.8) | copy-start | bytes 196612
  4.3 0.7 copy-start.4
  5.0 0.7 copy-start.5

commit v3 on v2

--- a/solution.py
+++ b/solution.py
@@ -28,9 +28,9 @@
 
 def kernel(
     members, shards,
-    latent_hbm, embed_hbm, source, area, target, w_query_hbm, w_keyval_hbm, w_head,
+    latent_hbm, embed_hbm, source_hbm, area_hbm, target_hbm, w_query_hbm, w_keyval_hbm, w_head_hbm,
     loss_out, d_latent, grad_query, grad_keyval, grad_head,
-    latent, embed, w_query, w_keyval, meta,
+    latent, embed, source, area, target, w_query, w_keyval, w_head, meta,
     lat3, lat4, lat_t, lat_z, table, query, q_norm, q_rstd, k_norm, k_rstd, expo, recip, mixed, hidden, d_hid,
     wh, preds, preds_in, ph, ph_in, ph_fin, part, part_in,
     own_dt, halo, halo_in, ob, dt4, dqs, dqs_in, pq, yq, zq, zq_in, dtz, pk, yk, fq, fk,
@@ -40,7 +40,10 @@
     loads = [
         pltpu.make_async_copy(src, dst, load_sem.at[i])
         for i, (src, dst) in enumerate(
-            ((latent_hbm, latent), (embed_hbm, embed), (w_query_hbm, w_query), (w_keyval_hbm, w_keyval))
+            (
+                (latent_hbm, latent), (embed_hbm, embed), (w_query_hbm, w_query), (source_hbm, source),
+                (area_hbm, area), (target_hbm, target), (w_head_hbm, w_head), (w_keyval_hbm, w_keyval),
+            )
         )
     ]
     for load in loads:
@@ -94,14 +97,15 @@
     lat3[3 * nodes :, :] = jnp.zeros((padded - 3 * nodes, width), BF)
     lat4[:nodes, :] = latent[...]
 
+    for load in loads[1:7]:
+        load.wait()
     wh[...] = jnp.zeros(wh.shape, BF)
     wh[:variables, :] = w_head[...]
     meta[...] = jnp.zeros(meta.shape, F32)
     meta[:variables, :] = target[...]
     meta[104:105, :] = area[...]
     meta[112 : 112 + source.shape[0], :] = source[...].astype(F32)
-    loads[1].wait()
-    loads[2].wait()
+
 
     def query_step(i, carry):
         cols = pl.ds(pl.multiple_of(i * 256, 256), 256)
@@ -139,7 +143,7 @@
 
     halo_up.wait()
     halo_down.wait()
-    loads[3].wait()
+    loads[7].wait()
 
     def table_step(i, carry):
         cols = pl.ds(pl.multiple_of(i * 256, 256), 256)
@@ -242,22 +246,76 @@
         - nhat * jnp.mean(d_normed * nhat, -1, keepdims=True)
     )
 
-    def dq_copy(c):
-        slot = lax.rem(c - m + members, members)
-        return send(dqs.at[c], dqs_in.at[slot], dq_sem, slot, c, s)
-
-    def halo_copies(c):
+    def dq_copies(t):
         return [
-            send(halo.at[0, c], halo_in.at[0, c], dth_sem, 2 * c, m, shard(shards - 1)),
-            send(halo.at[1, c], halo_in.at[1, c], dth_sem, 2 * c + 1, m, shard(1)),
+            send(dqs.at[t, member(i)], dqs_in.at[t, i], dq_sem, t * members + i, member(i), s)
+            for i in range(1, members)
         ]
 
-    for c in range(members):
-        for t in range(per_chunk):
-            p = c * per_chunk + t
+    def halo_copies(t):
+        return [
+            send(halo.at[0, t], halo_in.at[0, t], dth_sem, 2 * t, m, shard(shards - 1)),
+            send(halo.at[1, t], halo_in.at[1, t], dth_sem, 2 * t + 1, m, shard(1)),
+        ]
+
+    def dtm_copies(t):
+        return [
+            send(ob.at[t, member(i)], dt4.at[t, i], dtm_sem, t * members + i, member(i), s)
+            for i in range(1, members)
+        ]
+
+    def own_block(t):
+        for copy in halo_copies(t):
+            copy.wait()
+        ob[t] = (own_dt[t] + halo_in[0, t].astype(F32) + halo_in[1, t].astype(F32)).astype(BF)
+        for copy in dtm_copies(t):
+            copy.start()
+
+    def upward(t, slot):
+        return send(dtz.at[t, slot], dtz.at[t, slot], up_sem, t * outer + slot, m, 2 * (a + 1) + b)
+
+    def downward(t, slot):
+        return send(dtz.at[t, slot], dtz.at[t, slot], down_sem, t * outer + slot, m, 2 * (a - 1) + b)
+
+    def line_start(t):
+        dt4[t, 0] = ob[t, m]
+        for copy in dtm_copies(t):
+            copy.wait()
+        dtz[t, a] = dt4[t].reshape(held, 2 * LANES)
+
+        @pl.when(a < outer - 1)
+        def _():
+            upward(t, a).start()
+
+        @pl.when(a > 0)
+        def _():
+            downward(t, a).start()
+
+    def line_step(t, step):
+        @pl.when(a - step >= 0)
+        def _():
+            upward(t, a - step).wait_recv()
+
+            @pl.when(a < outer - 1)
+            def _():
+                upward(t, a - step).start()
+
+        @pl.when(a + step < outer)
+        def _():
+            downward(t, a + step).wait_recv()
+
+            @pl.when(a > 0)
+            def _():
+                downward(t, a + step).start()
+
+    for t in range(per_chunk):
+        for c in range(members):
+            p = t * members + c
+            if t > 0 and c == members // 2:
+                own_block(t - 1)
+            here = slice(0, LANES)
+            there = slice(LANES, 2 * LANES)
             cols = slice(p * LANES, (p + 1) * LANES)
-            here = slice(t * LANES, (t + 1) * LANES)
-            there = slice(chunk + t * LANES, chunk + (t + 1) * LANES)
             d_out = d_hid[:, cols] * recip[:, cols]
             d_outl = d_out.astype(BF)
             kn = k_norm[:, cols]
@@ -270,20 +328,18 @@
             qn = q_norm[:, cols]
             d_qn = mm(d_score, k2)
             qf = qn.astype(F32)
-            dqs[c, :, here] = (q_rstd[:, cols] * (d_qn - qf * head_mean(d_qn * qf))).astype(BF)
+            dqs[t, c] = (q_rstd[:, cols] * (d_qn - qf * head_mean(d_qn * qf))).astype(BF)
             d_kn = unstacked(mm_tn(d_score, qn))
             d_key = k_rstd[:, cols] * (d_kn - kn * head_mean(d_kn * kn))
             d_val = unstacked(mm_tn(e, d_outl))
             for where, grad in ((here, d_key), (there, d_val)):
-                halo[0, c, :, where] = grad[:nodes].astype(BF)
-                own_dt[c, :, where] = grad[nodes : 2 * nodes]
-                halo[1, c, :, where] = grad[2 * nodes : 3 * nodes].astype(BF)
-        for copy in halo_copies(c):
+                halo[0, t, c, :, where] = grad[:nodes].astype(BF)
+                own_dt[t, c, :, where] = grad[nodes : 2 * nodes]
+                halo[1, t, c, :, where] = grad[2 * nodes : 3 * nodes].astype(BF)
+        for copy in halo_copies(t) + dq_copies(t):
             copy.start()
-
-        @pl.when(c != m)
-        def _():
-            dq_copy(c).start()
+        if t > 0:
+            line_start(t - 1)
 
     total = part[...]
     for i in range(1, shards):
@@ -301,20 +357,16 @@
             recv_sem=hfin_sem.at[1, i], device_id=(member(i), s), device_id_type=MESH,
         ).start()
 
-    for c in range(members):
-        for copy in halo_copies(c):
+    last = per_chunk - 1
+    own_block(last)
+    dq_sums = []
+    for t in range(per_chunk):
+        dq_sum = dqs[t, m].astype(F32)
+        for i, copy in enumerate(dq_copies(t)):
             copy.wait()
-        ob[c] = (own_dt[c] + halo_in[0, c].astype(F32) + halo_in[1, c].astype(F32)).astype(BF)
-
-        @pl.when(c != m)
-        def _():
-            slot = lax.rem(c - m + members, members)
-            send(ob.at[c], dt4.at[slot], dtm_sem, slot, c, s).start()
-
-    dq_sum = dqs[m].astype(F32)
-    for i in range(1, members):
-        send(dqs.at[member(i)], dqs_in.at[i], dq_sem, i, member(i), s).wait()
-        dq_sum = dq_sum + dqs_in[i].astype(F32)
+            dq_sum = dq_sum + dqs_in[t, i + 1].astype(F32)
+        dq_sums.append(dq_sum)
+    dq_sum = jnp.concatenate(dq_sums, axis=1) if per_chunk > 1 else dq_sums[0]
     dq_sumb = dq_sum.astype(BF)
     for block in range(width // 256):
         piece = mm_tn(embed[:, block * 256 : (block + 1) * 256], dq_sumb) * scale
@@ -325,52 +377,23 @@
     y_query = send(pq.at[1 - b], yq, y_sem, 0, m, partner)
     y_query.start()
 
-    dt4[0] = ob[m]
-    for i in range(1, members):
-        send(ob.at[member(i)], dt4.at[i], dtm_sem, i, member(i), s).wait()
-    dtz[a] = dt4[...].reshape(held, 2 * chunk)
-
-    def upward(slot):
-        return send(dtz.at[slot], dtz.at[slot], up_sem, slot, m, 2 * (a + 1) + b)
-
-    def downward(slot):
-        return send(dtz.at[slot], dtz.at[slot], down_sem, slot, m, 2 * (a - 1) + b)
-
-    @pl.when(a < outer - 1)
-    def _():
-        upward(a).start()
-
-    @pl.when(a > 0)
-    def _():
-        downward(a).start()
+    line_start(last)
 
     d_lat = jnp.zeros((nodes, width), F32)
-    for c in range(members):
-        d_lat = d_lat + mm_nt(ob[c, :, :chunk], w_keyval[:, c * chunk : (c + 1) * chunk])
-        d_lat = d_lat + mm_nt(ob[c, :, chunk:], w_keyval[:, width + c * chunk : width + (c + 1) * chunk])
+    for p in range(pairs):
+        block = ob[p // members, p % members]
+        d_lat = d_lat + mm_nt(block[:, :LANES], w_keyval[:, p * LANES : (p + 1) * LANES])
+        d_lat = d_lat + mm_nt(
+            block[:, LANES:], w_keyval[:, width + p * LANES : width + (p + 1) * LANES]
+        )
     d_latent[...] = d_lat
 
     zq_copies = [
         send(zq.at[other(i)], zq_in.at[i], zq_sem, i, m, 2 * other(i) + b) for i in range(1, outer)
     ]
     for step in range(1, outer):
-
-        @pl.when(a - step >= 0)
-        def _():
-            upward(a - step).wait_recv()
-
-            @pl.when(a < outer - 1)
-            def _():
-                upward(a - step).start()
-
-        @pl.when(a + step < outer)
-        def _():
-            downward(a + step).wait_recv()
-
-            @pl.when(a > 0)
-            def _():
-                downward(a + step).start()
-
+        for t in range(per_chunk):
+            line_step(t, step)
         if step == 1:
             y_query.wait()
             zq[...] = (pq[b].astype(F32) + yq[...].astype(F32)).astype(BF)
@@ -379,9 +402,13 @@
 
     for copy in latz_copies:
         copy.wait()
-    acc = jnp.zeros((two, 2 * chunk), F32)
-    for t in range(outer):
-        acc = acc + mm(lat_z[t], dtz[t])
+    accs = []
+    for t in range(per_chunk):
+        acc = jnp.zeros((two, 2 * LANES), F32)
+        for x in range(outer):
+            acc = acc + mm(lat_z[x], dtz[t, x])
+        accs.append(acc)
+    acc = jnp.concatenate(accs, axis=1) if per_chunk > 1 else accs[0]
     acc = acc * scale
     pk[0] = acc[:out_rows]
     pk[1] = acc[out_rows:]
@@ -435,20 +462,25 @@
         copies[-1].wait()
         for i in range(1, chips):
             forward(buffer, sems, i).wait()
-    for c in range(members):
-        grad_query[:, c * chunk : (c + 1) * chunk] = fq[c]
-        grad_keyval[:, c * chunk : (c + 1) * chunk] = fk[c, :, :chunk]
-        grad_keyval[:, width + c * chunk : width + (c + 1) * chunk] = fk[c, :, chunk:]
-
-    for slot in range(outer):
-
-        @pl.when((a < outer - 1) & (a >= slot))
-        def _():
-            upward(slot).wait_send()
-
-        @pl.when((a > 0) & (a <= slot))
-        def _():
-            downward(slot).wait_send()
+    for p in range(pairs):
+        t, c = p // members, p % members
+        cols = slice(p * LANES, (p + 1) * LANES)
+        grad_query[:, cols] = fq[c, :, t * LANES : (t + 1) * LANES]
+        grad_keyval[:, cols] = fk[c, :, 2 * t * LANES : (2 * t + 1) * LANES]
+        grad_keyval[:, width + p * LANES : width + (p + 1) * LANES] = fk[
+            c, :, (2 * t + 1) * LANES : (2 * t + 2) * LANES
+        ]
+
+    for t in range(per_chunk):
+        for slot in range(outer):
+
+            @pl.when((a < outer - 1) & (a >= slot))
+            def _():
+                upward(t, slot).wait_send()
+
+            @pl.when((a > 0) & (a <= slot))
+            def _():
+                downward(t, slot).wait_send()
 
 
 def on_device(latent, grid_embed, edge_src, area, target, w_query, w_keyval, w_head):
@@ -462,6 +494,7 @@
     chunk = width // members
     outer = shards // 2
     pairs = width // LANES
+    groups = chunk // LANES
     padded = -(-3 * nodes // LANES) * LANES
     vm = pltpu.VMEM
     dma = lambda n: pltpu.SemaphoreType.DMA((2, n))
@@ -475,8 +508,12 @@
     scratch = [
         vm((nodes, width), BF),
         vm((rows, width), BF),
+        vm((edge_src.shape[1], rows), jnp.int32),
+        vm((1, rows), F32),
+        vm((variables, rows), F32),
         vm((width, width), BF),
         vm((width, 2 * width), BF),
+        vm((variables, width), BF),
         vm((LANES, rows), F32),
         vm((padded, width), BF),
         vm((held, width), BF),
@@ -501,37 +538,37 @@
         vm((members, out_rows, LANES), BF),
         vm((8, LANES), F32),
         vm((shards, 8, LANES), F32),
-        vm((members, nodes, 2 * chunk), F32),
-        vm((2, members, nodes, 2 * chunk), BF),
-        vm((2, members, nodes, 2 * chunk), BF),
-        vm((members, nodes, 2 * chunk), BF),
-        vm((members, nodes, 2 * chunk), BF),
-        vm((members, rows, chunk), BF),
-        vm((members, rows, chunk), BF),
+        vm((groups, members, nodes, 2 * LANES), F32),
+        vm((2, groups, members, nodes, 2 * LANES), BF),
+        vm((2, groups, members, nodes, 2 * LANES), BF),
+        vm((groups, members, nodes, 2 * LANES), BF),
+        vm((groups, members, nodes, 2 * LANES), BF),
+        vm((groups, members, rows, LANES), BF),
+        vm((groups, members, rows, LANES), BF),
         vm((2, outer, out_rows, chunk), BF),
         vm((outer, out_rows, chunk), BF),
         vm((outer, out_rows, chunk), BF),
         vm((outer, out_rows, chunk), BF),
-        vm((outer, held, 2 * chunk), BF),
+        vm((groups, outer, held, 2 * LANES), BF),
         vm((2, out_rows, 2 * chunk), F32),
         vm((out_rows, 2 * chunk), BF),
         vm((members, out_rows, chunk), BF),
         vm((members, out_rows, 2 * chunk), BF),
         dma(2), dma(members), dma(members), dma(shards), dma(shards), dma(members),
-        dma(2 * members), dma(members), dma(members),
-        dma(2), dma(outer), dma(outer), dma(outer), dma(outer), dma(members), dma(members),
-        pltpu.SemaphoreType.DMA((4,)),
+        dma(2 * groups), dma(groups * members), dma(groups * members),
+        dma(2), dma(outer), dma(outer), dma(groups * outer), dma(groups * outer), dma(members), dma(members),
+        pltpu.SemaphoreType.DMA((8,)),
     ]
     spec = pl.BlockSpec(memory_space=pltpu.VMEM)
-    hbm = pl.BlockSpec(memory_space=pl.ANY)
+    hbm = pl.BlockSpec(memory_space=pltpu.HBM)
     loss, d_lat, grad_q, grad_kv, grad_h = pl.pallas_call(
         functools.partial(kernel, members, shards),
         out_shape=outs,
-        in_specs=[hbm, hbm, spec, spec, spec, hbm, hbm, spec],
+        in_specs=[hbm] * 8,
         out_specs=tuple([spec] * 5),
         scratch_shapes=scratch,
         compiler_params=pltpu.CompilerParams(
-            collective_id=0, has_side_effects=True, vmem_limit_bytes=52 * 1024 * 1024
+            collective_id=0, has_side_effects=True, vmem_limit_bytes=63 * 1024 * 1024
         ),
     )(latent[0], grid_embed, edge_src.T, area[None], target.T, w_query, w_keyval, w_head.T)
     return loss[0], d_lat[None], grad_q.astype(F32), grad_kv.astype(F32), grad_h.T

time: 74.8 us -> 74 us (0.989)
  local copies, waits for them, and re-layouts: 6.34 us -> 3 us
  other arithmetic: 1.92 us -> 3.91 us
  Pallas kernels: 63.7 us -> 64.5 us
    unnamed x14 -> x2, local copies, waits for them, and re-layouts: 6.34 us -> 3 us
    convert_element_type x1, other arithmetic: 1.08 us -> 2.12 us  [on_device(): grad_kv.astype(F32)]
    convert_element_type x1, other arithmetic: 0.84 us -> 1.79 us  [on_device(): grad_q.astype(F32)]
    pallas_call x1, Pallas kernels: 63.7 us -> 64.5 us  [on_device(): pl.pallas_call(functools.partial(kernel, members, shards), out_shape=outs...]
where the time goes in v3:
time: 74 us; the launch traced here: 73.7 us
  Pallas kernels  64.5 us (87%)
  other arithmetic  3.91 us (5%)
  local copies, waits for them, and re-layouts  3 us (4%)
  between operations  2.33 us (3%)
    pallas_call x1, Pallas kernels, on_device(): pl.pallas_call(functools.partial(kernel, members, shards), out_shape=outs...  64.5 us
    unnamed x2, local copies, waits for them, and re-layouts  3 us
    convert_element_type x1, other arithmetic, on_device(): grad_kv.astype(F32)  2.12 us
    convert_element_type x1, other arithmetic, on_device(): grad_q.astype(F32)  1.79 us

profile of v3, /device:TPU:0, one launch (start us, length us, event | category | flops | bytes accessed | tf_op | source)
XLA Modules:
  0.0 73.7 jit_solution(15734378564137887352)
XLA Ops:
  0.6 64.5 %shard_map.119 = (f32[1,1]{1,0:T(1,128)}, f32[32,1024]{1,0:T(8,128)}, bf16[128,1024]{1,0:T(8,128)(2,1)}, bf16[128,2048]{1,0:T(8,128)(2,1)}, f32[100,128]{1,0:T(8,128)}) custom-call(bf16[32,1024]{1,0:T(8,128)(2,1)} %bitcast.11, bf16[256,1024]{1,0:T(8,128)(2,1)} %embed_hbm.1, s32[3,256]{1,0:T(4,128)} %bitcast.13, f32[1,256]{1,0:T(1,128)} %bitcast.14, ...), custom_call_target="tpu_custom_call" | custom-call | tf_op jit(solution)/shard_map/pallas_call | solution.py:564
  65.1 2.1 %convert_element_type.7 = f32[128,2048]{1,0:T(8,128)} convert(bf16[128,2048]{1,0:T(8,128)(2,1)} %get-tuple-element.13) | non-fusion elementwise | flops 262144 | bytes 1572864 | tf_op jit(solution)/shard_map/convert_element_type | solution.py:574
  67.3 1.8 %convert_element_type.6 = f32[128,1024]{1,0:T(8,128)} convert(bf16[128,1024]{1,0:T(8,128)(2,1)} %get-tuple-element.12) | non-fusion elementwise | flops 131072 | bytes 786432 | tf_op jit(solution)/shard_map/convert_element_type | solution.py:574
  69.6 1.6 %copy.17 = f32[1,32,1024]{2,1,0:T(8,128)} copy(f32[1,32,1024]{2,1,0:T(8,128)} %bitcast.9) | data formatting | bytes 262144
  71.2 1.4 %copy.18 = f32[128,100]{0,1:T(8,128)} copy(f32[128,100]{0,1:T(8,128)} %bitcast.12) | data formatting | bytes 102400
